TPU v7x, 128 devices: a whole 4x4x4 slice. The times are simulated.
128 devices in a mesh: seq: 32 (over y, z, core), chan: 4 (over x).
Axes of the slice: x: 4, y: 4, z: 4, core: 2. Of those that a mesh axis runs over, the one named last changes fastest.
Arguments:
- streams: bfloat16 [3, 256, 32768], P(None, 'chan', 'seq'), may hold values from -6 to 6
- short_taps: float32 [3, 256, 3], P(None, 'chan'), may hold values from -3 to 3
- long_filter: float32 [256, 32768], P('chan', 'seq'), may hold values from -0.03125 to 0.03125
- skip_gain: float32 [256], P('chan'), may hold values from -4 to 4
Outputs:
- gated: bfloat16 [256, 32768], P('chan', 'seq')
All inputs are finite; a program needn't handle non-finite values.
Results may differ from a plain program's by a relative error of at most 0.001.
Values may be sent and summed in bfloat16 or wider, within the bound.
A program may use at most 64 MiB of HBM per device.

v0:
```python
import functools
import math

import jax
import jax.numpy as jnp
import ml_dtypes
import numpy as np
from jax import lax
from jax.experimental import pallas as pl
from jax.experimental.pallas import tpu as pltpu
from jax.sharding import PartitionSpec as P

LANES = 128
OWN = 2


def halves(table):
    high = table.astype(ml_dtypes.bfloat16)
    low = (table - high.astype(np.float64)).astype(ml_dtypes.bfloat16)
    return np.stack([high, low])


def tables(rows):
    row = np.arange(rows)
    lane = np.arange(LANES)
    angle = (2.0 * math.pi / (4 * rows)) * ((2 * row[:, None] + 1) * row[None, :] % (4 * rows))
    outer = np.concatenate([np.cos(angle), -np.sin(angle)], axis=0)
    outer_back = outer.T / (rows * LANES)
    angle = (2.0 * math.pi / LANES) * (lane[:, None] * lane[None, :] % LANES)
    cos, sin = np.cos(angle), np.sin(angle)
    inner = np.block([[cos, -sin], [sin, cos]])
    angle = (2.0 * math.pi / (4 * rows * LANES)) * ((2 * row[:, None] + 1) * lane[None, :])
    turn = np.stack([np.cos(angle), np.sin(angle)]).astype(np.float32)
    return halves(outer), halves(outer_back), np.concatenate([halves(inner), halves(inner.T)]), turn


def split(x):
    high = x.astype(jnp.bfloat16)
    return high, (x - high.astype(jnp.float32)).astype(jnp.bfloat16)


def dot(a, b):
    return jnp.dot(a, b, preferred_element_type=jnp.float32)


def left(table, x):
    high, low = split(x)
    return dot(table[0], high) + dot(table[0], low) + dot(table[1], high)


def right(x, high_table, low_table):
    high, low = split(x)
    return dot(high, high_table) + dot(low, high_table) + dot(high, low_table)


def forward(x, rows, outer, inner, turn):
    part = left(outer, x)
    cos, sin = turn[0], turn[1]
    turned = []
    for c in range(OWN):
        re = part[:rows, c * LANES:(c + 1) * LANES]
        im = part[rows:, c * LANES:(c + 1) * LANES]
        turned.append(jnp.concatenate([re * cos + im * sin, im * cos - re * sin], axis=1))
    return right(jnp.concatenate(turned, axis=0), inner[0], inner[1])


def backward(y, rows, outer_back, inner, turn):
    part = right(y, inner[2], inner[3])
    cos, sin = turn[0], turn[1]
    re_parts, im_parts = [], []
    for c in range(OWN):
        re = part[c * rows:(c + 1) * rows, :LANES]
        im = part[c * rows:(c + 1) * rows, LANES:]
        re_parts.append(re * cos - im * sin)
        im_parts.append(im * cos + re * sin)
    turned = jnp.concatenate(
        [jnp.concatenate(re_parts, axis=1), jnp.concatenate(im_parts, axis=1)], axis=0
    )
    return left(outer_back, turned)


def multiply(a, b):
    a_re, a_im, b_re, b_im = a[:, :LANES], a[:, LANES:], b[:, :LANES], b[:, LANES:]
    return jnp.concatenate([a_re * b_re - a_im * b_im, a_re * b_im + a_im * b_re], axis=1)


def short_conv(x, taps, lane, first):
    one = pltpu.roll(x, 1, 1)
    two = pltpu.roll(x, 2, 1)
    one_up = jnp.where(first, 0.0, pltpu.roll(one, 1, 0))
    two_up = jnp.where(first, 0.0, pltpu.roll(two, 1, 0))
    one = jnp.where(lane < 1, one_up, one)
    two = jnp.where(lane < 2, two_up, two)
    return taps[0] * x + taps[1] * one + taps[2] * two


def kernel(
    peers, streams_hbm, filter_hbm, taps_ref, skip_ref, outer_hbm, back_hbm, inner_hbm, turn_hbm,
    out_ref,
    streams, filt, outer, back, inner, turn,
    filter_out, filter_in, wide, pair_out, pair_in, query_out, query_in, gated_out, gated_in,
    load_sem, send_sem, recv_sem,
):
    rows = 8 * peers
    channels = OWN * peers
    me = lax.axis_index("seq")
    barrier = pltpu.get_barrier_semaphore()

    def load(i, source, target):
        copy = pltpu.make_async_copy(source, target, load_sem.at[i])
        copy.start()
        return copy

    filter_load = load(0, filter_hbm, filt)
    streams_load = load(1, streams_hbm, streams)
    table_loads = [
        load(2, outer_hbm, outer), load(3, turn_hbm, turn), load(4, inner_hbm, inner), load(5, back_hbm, back)
    ]

    def each_peer(step):
        def turn_to(d, carry):
            step(lax.rem(me + d, peers))
            return carry

        lax.fori_loop(1, peers, turn_to, 0)

    def greet(peer):
        pl.semaphore_signal(
            barrier, inc=1, device_id={"seq": peer}, device_id_type=pl.DeviceIdType.MESH
        )

    each_peer(greet)

    def send(source, target, index):
        def to(peer):
            pltpu.make_async_remote_copy(
                src_ref=source.at[peer],
                dst_ref=target.at[me],
                send_sem=send_sem.at[index],
                recv_sem=recv_sem.at[index],
                device_id={"seq": peer},
                device_id_type=pl.DeviceIdType.MESH,
            ).start()

        each_peer(to)
        target[me] = source[me]

    def wait(buffer, sem):
        others = buffer.at[pl.ds(0, peers - 1)]
        pltpu.make_async_copy(others, others, sem).wait()

    def regroup(values, target):
        for t in range(8):
            wide[pl.ds(t, channels, stride=8), :] = values(t)
        target(wide[...].reshape(peers, OWN * 8, LANES))

    filter_load.wait()

    def put_filter(v):
        filter_out[...] = v

    regroup(lambda t: filt[:, t * LANES:(t + 1) * LANES], put_filter)
    pl.semaphore_wait(barrier, peers - 1)
    send(filter_out, filter_in, 0)

    streams_load.wait()

    def stream(s):
        return lambda t: streams[s, :, t * LANES:(t + 1) * LANES].astype(jnp.float32)

    def put_pair(s):
        def put(v):
            pair_out[:, s * 16:(s + 1) * 16, :] = v.astype(jnp.bfloat16)

        return put

    regroup(stream(1), put_pair(0))
    regroup(stream(2), put_pair(1))
    send(pair_out, pair_in, 1)

    def put_query(v):
        query_out[...] = v.astype(jnp.bfloat16)

    regroup(stream(0), put_query)
    send(query_out, query_in, 2)

    for copy in table_loads:
        copy.wait()
    wait(filter_in, recv_sem.at[0])

    def by_channel(v):
        parts = [v[:, 8 * c:8 * c + 8, :].reshape(rows, LANES) for c in range(OWN)]
        return jnp.concatenate(parts, axis=1)

    filter_bins = forward(by_channel(filter_in[...]), rows, outer, inner, turn)

    lane = lax.broadcasted_iota(jnp.int32, (rows, LANES), 1)
    first = lax.broadcasted_iota(jnp.int32, (rows, LANES), 0) < 1

    def shorted(v, s, c):
        own = OWN * me + c
        taps = [taps_ref[(s * channels + own) * 3 + i] for i in range(3)]
        return short_conv(v[:, 8 * c:8 * c + 8, :].reshape(rows, LANES), taps, lane, first)

    wait(pair_in, recv_sem.at[1])
    key = pair_in[:, 0:16, :].astype(jnp.float32)
    value = pair_in[:, 16:32, :].astype(jnp.float32)
    mixed = jnp.concatenate(
        [shorted(key, 1, c) * shorted(value, 2, c) for c in range(OWN)], axis=1
    )
    bins = forward(mixed, rows, outer, inner, turn)
    conv = backward(multiply(bins, filter_bins), rows, back, inner, turn)

    wait(query_in, recv_sem.at[2])
    query = query_in[...].astype(jnp.float32)
    results = []
    for c in range(OWN):
        cut = slice(c * LANES, (c + 1) * LANES)
        gated = shorted(query, 0, c) * (conv[:, cut] + skip_ref[OWN * me + c] * mixed[:, cut])
        results.append(gated.reshape(peers, 8, LANES))
    gated_out[...] = jnp.concatenate(results, axis=1).astype(jnp.bfloat16)
    send(gated_out, gated_in, 3)

    wait(filter_out, send_sem.at[0])
    wait(pair_out, send_sem.at[1])
    wait(query_out, send_sem.at[2])
    wait(gated_in, recv_sem.at[3])
    wide[...] = gated_in[...].astype(jnp.float32).reshape(peers * OWN * 8, LANES)
    for t in range(8):
        out_ref[:, t * LANES:(t + 1) * LANES] = wide[pl.ds(t, channels, stride=8), :].astype(jnp.bfloat16)
    wait(gated_out, send_sem.at[3])


def body(streams, short_taps, long_filter, skip_gain):
    peers = lax.axis_size("seq")
    rows = 8 * peers
    outer, back, inner, turn = (jnp.asarray(t) for t in tables(rows))
    anywhere = pl.BlockSpec(memory_space=pl.ANY)
    scalars = pl.BlockSpec(memory_space=pltpu.SMEM)
    f32, bf16 = jnp.float32, jnp.bfloat16
    one = (peers, OWN * 8, LANES)
    two = (peers, 2 * OWN * 8, LANES)
    vmem = pltpu.VMEM
    return pl.pallas_call(
        functools.partial(kernel, peers),
        out_shape=jax.ShapeDtypeStruct(long_filter.shape, bf16),
        in_specs=[anywhere, anywhere, scalars, scalars] + [anywhere] * 4,
        out_specs=pl.BlockSpec(memory_space=pltpu.VMEM),
        scratch_shapes=[
            vmem(streams.shape, bf16), vmem(long_filter.shape, f32),
            vmem(outer.shape, bf16), vmem(back.shape, bf16), vmem(inner.shape, bf16), vmem(turn.shape, f32),
            vmem(one, f32), vmem(one, f32), vmem((peers * OWN * 8, LANES), f32),
            vmem(two, bf16), vmem(two, bf16), vmem(one, bf16), vmem(one, bf16), vmem(one, bf16), vmem(one, bf16),
            pltpu.SemaphoreType.DMA((6,)), pltpu.SemaphoreType.DMA((4,)), pltpu.SemaphoreType.DMA((4,)),
        ],
        compiler_params=pltpu.CompilerParams(
            collective_id=0, has_side_effects=True, vmem_limit_bytes=48 * 1024 * 1024
        ),
    )(streams, long_filter, short_taps.reshape(-1), skip_gain, outer, back, inner, turn)


def solution(mesh):
    return jax.shard_map(
        body,
        mesh=mesh,
        in_specs=(P(None, "chan", "seq"), P(None, "chan", None), P("chan", "seq"), P("chan")),
        out_specs=P("chan", "seq"),
        check_vma=False,
    )
```

profile of v0, /device:TPU:1, one launch (start us, length us, event | category | flops | bytes accessed | tf_op | source)
XLA Modules:
  0.0 34.6 jit_solution(5592415542071688691)
XLA Ops:
  0.0 0.8 %copy.9 = f32[3,64,3]{2,1,0:T(8,128)S(1)} copy(f32[3,64,3]{1,2,0:T(4,128)} %param.9) | data formatting | bytes 4608 | tf_op args[1]
  0.8 0.0 copy-start.6
  0.8 0.2 reshape.3.taps_ref
  1.0 0.4 %copy-done.6 = f32[64]{0:T(128)S(1)} copy-done((f32[64]{0:T(128)S(1)}, f32[64]{0:T(128)}, u32[]{:S(2)}) %copy-start.6) | copy-done | bytes 280
  1.5 0.0 copy-start
  1.5 1.0 %copy-done = bf16[4,256,256]{2,1,0:T(8,128)(2,1)S(1)} copy-done((bf16[4,256,256]{2,1,0:T(8,128)(2,1)S(1)}, bf16[4,256,256]{2,1,0:T(8,128)(2,1)}, u32[]{:S(2)}) %copy-start) | copy-done | bytes 524312
  2.5 0.0 copy-start.1
  2.5 1.0 %copy-done.1 = bf16[2,256,512]{2,1,0:T(8,128)(2,1)S(1)} copy-done((bf16[2,256,512]{2,1,0:T(8,128)(2,1)S(1)}, bf16[2,256,512]{2,1,0:T(8,128)(2,1)}, u32[]{:S(2)}) %copy-start.1) | copy-done | bytes 524312
  3.5 0.0 copy-start.2
  3.5 1.0 %copy-done.2 = bf16[2,512,256]{2,1,0:T(8,128)(2,1)S(1)} copy-done((bf16[2,512,256]{2,1,0:T(8,128)(2,1)S(1)}, bf16[2,512,256]{2,1,0:T(8,128)(2,1)}, u32[]{:S(2)}) %copy-start.2) | copy-done | bytes 524312
  4.6 0.0 copy-start.3
  4.6 1.0 %copy-done.3 = bf16[3,64,1024]{2,1,0:T(8,128)(2,1)S(1)} copy-done((bf16[3,64,1024]{2,1,0:T(8,128)(2,1)S(1)}, bf16[3,64,1024]{2,1,0:T(8,128)(2,1)}, u32[]{:S(2)}) %copy-start.3) | copy-done | bytes 393240
  5.6 0.0 copy-start.4
  5.6 0.9 %copy-done.4 = f32[64,1024]{1,0:T(8,128)S(1)} copy-done((f32[64,1024]{1,0:T(8,128)S(1)}, f32[64,1024]{1,0:T(8,128)}, u32[]{:S(2)}) %copy-start.4) | copy-done | bytes 262168
  6.5 0.0 copy-start.5
  6.5 0.9 %copy-done.5 = f32[2,256,128]{2,1,0:T(8,128)S(1)} copy-done((f32[2,256,128]{2,1,0:T(8,128)S(1)}, f32[2,256,128]{2,1,0:T(8,128)}, u32[]{:S(2)}) %copy-start.5) | copy-done | bytes 262168
  7.5 26.4 %shard_map.82 = bf16[64,1024]{1,0:T(8,128)(2,1)S(1)} custom-call(bf16[3,64,1024]{2,1,0:T(8,128)(2,1)S(1)} %copy-done.3, f32[64,1024]{1,0:T(8,128)S(1)} %copy-done.4, f32[576]{0:T(1024)S(1)} %reshape.3.taps_ref, f32[64]{0:T(128)S(1)} %copy-done.6, bf16[2,512,256]{2,1,0:T(8,128)(2,1)S(1)} %copy-done.2, bf16[2,256,512]{2,1,0:T(8,128)(2,1)S(1)} %copy-done.1, ...), custom_call_target="tpu_custom_call" | custom-call | tf_op jit(solution)/shard_map/pallas_call | solution.py:244
  33.9 0.7 %copy.11 = bf16[64,1024]{1,0:T(8,128)(2,1)} copy(bf16[64,1024]{1,0:T(8,128)(2,1)S(1)} %shard_map.82) | data formatting | bytes 262144
Async XLA Ops:
  0.8 0.7 %copy-start.6 = (f32[64]{0:T(128)S(1)}, f32[64]{0:T(128)}, u32[]{:S(2)}) copy-start(f32[64]{0:T(128)} %skip_ref.1) | copy-start | bytes 772
  1.5 1.0 %copy-start = (bf16[4,256,256]{2,1,0:T(8,128)(2,1)S(1)}, bf16[4,256,256]{2,1,0:T(8,128)(2,1)}, u32[]{:S(2)}) copy-start(bf16[4,256,256]{2,1,0:T(8,128)(2,1)} %constant.10.clone.inner_hbm) | copy-start | bytes 1572868
  2.5 1.0 %copy-start.1 = (bf16[2,256,512]{2,1,0:T(8,128)(2,1)S(1)}, bf16[2,256,512]{2,1,0:T(8,128)(2,1)}, u32[]{:S(2)}) copy-start(bf16[2,256,512]{2,1,0:T(8,128)(2,1)} %constant.9.clone.back_hbm) | copy-start | bytes 1572868
  3.5 1.0 %copy-start.2 = (bf16[2,512,256]{2,1,0:T(8,128)(2,1)S(1)}, bf16[2,512,256]{2,1,0:T(8,128)(2,1)}, u32[]{:S(2)}) copy-start(bf16[2,512,256]{2,1,0:T(8,128)(2,1)} %constant.8.clone.outer_hbm) | copy-start | bytes 1572868
  4.6 1.0 %copy-start.3 = (bf16[3,64,1024]{2,1,0:T(8,128)(2,1)S(1)}, bf16[3,64,1024]{2,1,0:T(8,128)(2,1)}, u32[]{:S(2)}) copy-start(bf16[3,64,1024]{2,1,0:T(8,128)(2,1)} %streams_hbm.1) | copy-start | bytes 1179652
  5.6 0.9 %copy-start.4 = (f32[64,1024]{1,0:T(8,128)S(1)}, f32[64,1024]{1,0:T(8,128)}, u32[]{:S(2)}) copy-start(f32[64,1024]{1,0:T(8,128)} %filter_hbm.1) | copy-start | bytes 786436
  6.5 0.9 %copy-start.5 = (f32[2,256,128]{2,1,0:T(8,128)S(1)}, f32[2,256,128]{2,1,0:T(8,128)}, u32[]{:S(2)}) copy-start(f32[2,256,128]{2,1,0:T(8,128)} %constant.11.clone.turn_hbm) | copy-start | bytes 786436
where the time goes:
time: 35 us; the launch traced here: 34.6 us
  Pallas kernels  26.4 us (75%)
  local copies, waits for them, and re-layouts  8.12 us (23%)
    pallas_call x1, Pallas kernels, body(): pl.pallas_call(functools.partial(kernel, peers), out_shape=jax.ShapeDtype...  26.4 us
    unnamed x16, local copies, waits for them, and re-layouts  7.92 us

commit v1 on v0

--- a/solution.py
+++ b/solution.py
@@ -12,6 +12,7 @@
 
 LANES = 128
 OWN = 2
+VMEM_LIMIT = 60 * 1024 * 1024
 
 
 def halves(table):
@@ -95,9 +96,9 @@
 
 
 def kernel(
-    peers, streams_hbm, filter_hbm, taps_ref, skip_ref, outer_hbm, back_hbm, inner_hbm, turn_hbm,
+    peers, streams_hbm, filter_hbm, taps_hbm, skip_hbm, outer_hbm, back_hbm, inner_hbm, turn_hbm,
     out_ref,
-    streams, filt, outer, back, inner, turn,
+    streams, filt, taps_v, skip_v, outer, back, inner, turn,
     filter_out, filter_in, wide, pair_out, pair_in, query_out, query_in, gated_out, gated_in,
     load_sem, send_sem, recv_sem,
 ):
@@ -114,7 +115,8 @@
     filter_load = load(0, filter_hbm, filt)
     streams_load = load(1, streams_hbm, streams)
     table_loads = [
-        load(2, outer_hbm, outer), load(3, turn_hbm, turn), load(4, inner_hbm, inner), load(5, back_hbm, back)
+        load(2, outer_hbm, outer), load(3, turn_hbm, turn), load(4, inner_hbm, inner), load(5, back_hbm, back),
+        load(6, taps_hbm, taps_v), load(7, skip_hbm, skip_v),
     ]
 
     def each_peer(step):
@@ -197,9 +199,14 @@
     lane = lax.broadcasted_iota(jnp.int32, (rows, LANES), 1)
     first = lax.broadcasted_iota(jnp.int32, (rows, LANES), 0) < 1
 
+    channel = lax.broadcasted_iota(jnp.int32, (1, channels), 1)
+
+    def pick(v, own):
+        return jnp.sum(jnp.where(channel == own, v, 0.0), axis=1, keepdims=True)
+
     def shorted(v, s, c):
         own = OWN * me + c
-        taps = [taps_ref[(s * channels + own) * 3 + i] for i in range(3)]
+        taps = [pick(taps_v[s, i:i + 1, :], own) for i in range(3)]
         return short_conv(v[:, 8 * c:8 * c + 8, :].reshape(rows, LANES), taps, lane, first)
 
     wait(pair_in, recv_sem.at[1])
@@ -216,7 +223,7 @@
     results = []
     for c in range(OWN):
         cut = slice(c * LANES, (c + 1) * LANES)
-        gated = shorted(query, 0, c) * (conv[:, cut] + skip_ref[OWN * me + c] * mixed[:, cut])
+        gated = shorted(query, 0, c) * (conv[:, cut] + pick(skip_v[...], OWN * me + c) * mixed[:, cut])
         results.append(gated.reshape(peers, 8, LANES))
     gated_out[...] = jnp.concatenate(results, axis=1).astype(jnp.bfloat16)
     send(gated_out, gated_in, 3)
@@ -236,27 +243,29 @@
     rows = 8 * peers
     outer, back, inner, turn = (jnp.asarray(t) for t in tables(rows))
     anywhere = pl.BlockSpec(memory_space=pl.ANY)
-    scalars = pl.BlockSpec(memory_space=pltpu.SMEM)
     f32, bf16 = jnp.float32, jnp.bfloat16
     one = (peers, OWN * 8, LANES)
     two = (peers, 2 * OWN * 8, LANES)
     vmem = pltpu.VMEM
+    taps = jnp.transpose(short_taps, (0, 2, 1))
+    skip = skip_gain.reshape(1, -1)
     return pl.pallas_call(
         functools.partial(kernel, peers),
         out_shape=jax.ShapeDtypeStruct(long_filter.shape, bf16),
-        in_specs=[anywhere, anywhere, scalars, scalars] + [anywhere] * 4,
+        in_specs=[anywhere] * 8,
         out_specs=pl.BlockSpec(memory_space=pltpu.VMEM),
         scratch_shapes=[
             vmem(streams.shape, bf16), vmem(long_filter.shape, f32),
+            vmem(taps.shape, f32), vmem(skip.shape, f32),
             vmem(outer.shape, bf16), vmem(back.shape, bf16), vmem(inner.shape, bf16), vmem(turn.shape, f32),
             vmem(one, f32), vmem(one, f32), vmem((peers * OWN * 8, LANES), f32),
             vmem(two, bf16), vmem(two, bf16), vmem(one, bf16), vmem(one, bf16), vmem(one, bf16), vmem(one, bf16),
-            pltpu.SemaphoreType.DMA((6,)), pltpu.SemaphoreType.DMA((4,)), pltpu.SemaphoreType.DMA((4,)),
+            pltpu.SemaphoreType.DMA((8,)), pltpu.SemaphoreType.DMA((4,)), pltpu.SemaphoreType.DMA((4,)),
         ],
         compiler_params=pltpu.CompilerParams(
-            collective_id=0, has_side_effects=True, vmem_limit_bytes=48 * 1024 * 1024
+            collective_id=0, has_side_effects=True, vmem_limit_bytes=VMEM_LIMIT
         ),
-    )(streams, long_filter, short_taps.reshape(-1), skip_gain, outer, back, inner, turn)
+    )(streams, long_filter, taps, skip, outer, back, inner, turn)
 
 
 def solution(mesh):

time: 35 us -> 27.9 us (0.80)
  local copies, waits for them, and re-layouts: 8.12 us -> 1.57 us
    unnamed x16 -> x1, local copies, waits for them, and re-layouts: 7.92 us -> 1.57 us
where the time goes in v1:
time: 27.9 us; the launch traced here: 27.8 us
  Pallas kernels  26.2 us (94%)
  local copies, waits for them, and re-layouts  1.57 us (6%)
    pallas_call x1, Pallas kernels, body(): pl.pallas_call(functools.partial(kernel, peers), out_shape=jax.ShapeDtype...  26.2 us
    unnamed x1, local copies, waits for them, and re-layouts  1.57 us

profile of v1, /device:TPU:1, one launch (start us, length us, event | category | flops | bytes accessed | tf_op | source)
XLA Modules:
  0.0 27.8 jit_solution(8262349178430001723)
XLA Ops:
  0.0 26.2 %shard_map.82 = bf16[64,1024]{1,0:T(8,128)(2,1)} custom-call(bf16[3,64,1024]{2,1,0:T(8,128)(2,1)} %streams_hbm.1, f32[64,1024]{1,0:T(8,128)} %filter_hbm.1, f32[3,3,64]{2,1,0:T(4,128)} %bitcast.2, f32[1,64]{1,0:T(1,128)} %bitcast.3, bf16[2,512,256]{2,1,0:T(8,128)(2,1)} %constant.8.clone.outer_hbm, bf16[2,256,512]{2,1,0:T(8,128)(2,1)} %constant.9.clone.back_hbm, ...), custom_call_target="tpu_custom_call" | custom-call | tf_op jit(solution)/shard_map/pallas_call | solution.py:252
  26.2 1.6 %copy.10 = bf16[64,1024]{1,0:T(8,128)(2,1)} copy(bf16[64,1024]{1,0:T(8,128)(2,1)} %shard_map.82) | data formatting | bytes 262144

commit v2 on v1

--- a/solution.py
+++ b/solution.py
@@ -12,7 +12,7 @@
 
 LANES = 128
 OWN = 2
-VMEM_LIMIT = 60 * 1024 * 1024
+VMEM_LIMIT = 48 * 1024 * 1024
 
 
 def halves(table):
@@ -33,6 +33,12 @@
     angle = (2.0 * math.pi / (4 * rows * LANES)) * ((2 * row[:, None] + 1) * lane[None, :])
     turn = np.stack([np.cos(angle), np.sin(angle)]).astype(np.float32)
     return halves(outer), halves(outer_back), np.concatenate([halves(inner), halves(inner.T)]), turn
+
+
+def far_first(peers):
+    steps = [(y, z, core) for y in range(max(1, peers // 8)) for z in range(min(4, peers // 2)) for core in range(2)]
+    hops = lambda step: min(step[0], 4 - step[0]) + min(step[1], 4 - step[1])
+    return sorted(steps[1:], key=hops, reverse=True)
 
 
 def split(x):
@@ -119,12 +125,13 @@
         load(6, taps_hbm, taps_v), load(7, skip_hbm, skip_v),
     ]
 
+    ring_at = [lax.rem(me // 8 + d, 4) * 8 for d in range(4)]
+    column_at = [lax.rem(me // 2 % 4 + d, 4) * 2 for d in range(4)]
+    core_at = [lax.rem(me % 2 + d, 2) for d in range(2)]
+
     def each_peer(step):
-        def turn_to(d, carry):
-            step(lax.rem(me + d, peers))
-            return carry
-
-        lax.fori_loop(1, peers, turn_to, 0)
+        for y, z, core in far_first(peers):
+            step(ring_at[y] + column_at[z] + core_at[core])
 
     def greet(peer):
         pl.semaphore_signal(
@@ -249,9 +256,10 @@
     vmem = pltpu.VMEM
     taps = jnp.transpose(short_taps, (0, 2, 1))
     skip = skip_gain.reshape(1, -1)
+    operands = (streams, long_filter, taps, skip, outer, back, inner, turn)
     return pl.pallas_call(
         functools.partial(kernel, peers),
-        out_shape=jax.ShapeDtypeStruct(long_filter.shape, bf16),
+        out_shape=vmem(long_filter.shape, bf16),
         in_specs=[anywhere] * 8,
         out_specs=pl.BlockSpec(memory_space=pltpu.VMEM),
         scratch_shapes=[
@@ -265,7 +273,7 @@
         compiler_params=pltpu.CompilerParams(
             collective_id=0, has_side_effects=True, vmem_limit_bytes=VMEM_LIMIT
         ),
-    )(streams, long_filter, taps, skip, outer, back, inner, turn)
+    )(*(pltpu.with_memory_space_constraint(x, pltpu.HBM) for x in operands))
 
 
 def solution(mesh):

time: 27.9 us -> 25.1 us (0.90)
  Pallas kernels: 26.2 us -> 24.3 us
  local copies, waits for them, and re-layouts: 1.57 us -> 0.66 us
    pallas_call x1, Pallas kernels: 26.2 us -> 24.3 us  [body(): pl.pallas_call(functools.partial(kernel, peers), out_shape=vmem(long_filt...]
    unnamed x1, local copies, waits for them, and re-layouts: 1.57 us -> 0.66 us
where the time goes in v2:
time: 25.1 us; the launch traced here: 24.9 us
  Pallas kernels  24.3 us (97%)
  local copies, waits for them, and re-layouts  0.66 us (3%)
    pallas_call x1, Pallas kernels, body(): pl.pallas_call(functools.partial(kernel, peers), out_shape=vmem(long_filt...  24.3 us
    unnamed x1, local copies, waits for them, and re-layouts  0.66 us

profile of v2, /device:TPU:1, one launch (start us, length us, event | category | flops | bytes accessed | tf_op | source)
XLA Modules:
  0.0 24.9 jit_solution(3990917651301238377)
XLA Ops:
  0.0 24.3 %shard_map.82 = bf16[64,1024]{1,0:T(8,128)(2,1)S(1)} custom-call(bf16[3,64,1024]{2,1,0:T(8,128)(2,1)} %streams_hbm.1, f32[64,1024]{1,0:T(8,128)} %filter_hbm.1, f32[3,3,64]{2,1,0:T(4,128)} %bitcast.2, f32[1,64]{1,0:T(1,128)} %bitcast.3, bf16[2,512,256]{2,1,0:T(8,128)(2,1)} %constant.8.clone.outer_hbm, bf16[2,256,512]{2,1,0:T(8,128)(2,1)} %constant.9.clone.back_hbm, ...), custom_call_target="tpu_custom_call" | custom-call | tf_op jit(solution)/shard_map/pallas_call | solution.py:260
  24.3 0.7 %copy.10 = bf16[64,1024]{1,0:T(8,128)(2,1)} copy(bf16[64,1024]{1,0:T(8,128)(2,1)S(1)} %shard_map.82) | data formatting | bytes 262144

commit v3 on v2

v3 whole, which is shorter than its diff:
```python
import functools
import math

import jax
import jax.numpy as jnp
import ml_dtypes
import numpy as np
from jax import lax
from jax.experimental import pallas as pl
from jax.experimental.pallas import tpu as pltpu
from jax.sharding import PartitionSpec as P

LANES = 128
OWN = 2
VMEM_LIMIT = 48 * 1024 * 1024


def halves(table):
    high = table.astype(ml_dtypes.bfloat16)
    low = (table - high.astype(np.float64)).astype(ml_dtypes.bfloat16)
    return np.stack([high, low])


def tables(rows):
    row = np.arange(rows)
    lane = np.arange(LANES)
    angle = (2.0 * math.pi / (4 * rows)) * ((2 * row[:, None] + 1) * row[None, :] % (4 * rows))
    outer = np.concatenate([np.cos(angle), -np.sin(angle)], axis=0)
    outer_back = outer.T / (rows * LANES)
    angle = (2.0 * math.pi / LANES) * (lane[:, None] * lane[None, :] % LANES)
    cos, sin = np.cos(angle), np.sin(angle)
    inner = np.block([[cos, -sin], [sin, cos]])
    angle = (2.0 * math.pi / (4 * rows * LANES)) * ((2 * row[:, None] + 1) * lane[None, :])
    turn = np.stack([np.cos(angle), np.sin(angle)]).astype(np.float32)
    return halves(outer), halves(outer_back), np.concatenate([halves(inner), halves(inner.T)]), turn


def far_first(peers):
    steps = [(y, z, core) for y in range(max(1, peers // 8)) for z in range(min(4, peers // 2)) for core in range(2)]
    hops = lambda step: min(step[0], 4 - step[0]) + min(step[1], 4 - step[1])
    return sorted(steps[1:], key=hops, reverse=True)


def split(x):
    high = x.astype(jnp.bfloat16)
    return high, (x - high.astype(jnp.float32)).astype(jnp.bfloat16)


def dot(a, b):
    return jnp.dot(a, b, preferred_element_type=jnp.float32)


def left(table, x):
    high, low = split(x)
    return dot(table[0], high) + dot(table[0], low) + dot(table[1], high)


def right(x, high_table, low_table):
    high, low = split(x)
    return dot(high, high_table) + dot(low, high_table) + dot(high, low_table)


def forward(x, rows, outer, inner, turn):
    part = left(outer, x)
    cos, sin = turn[0], turn[1]
    turned = []
    for c in range(OWN):
        re = part[:rows, c * LANES:(c + 1) * LANES]
        im = part[rows:, c * LANES:(c + 1) * LANES]
        turned.append(jnp.concatenate([re * cos + im * sin, im * cos - re * sin], axis=1))
    return right(jnp.concatenate(turned, axis=0), inner[0], inner[1])


def backward(y, rows, outer_back, inner, turn, turned):
    part = right(y, inner[2], inner[3])
    cos, sin = turn[0], turn[1]
    for c in range(OWN):
        lanes = slice(c * LANES, (c + 1) * LANES)
        re = part[c * rows:(c + 1) * rows, :LANES]
        im = part[c * rows:(c + 1) * rows, LANES:]
        turned[0, :rows, lanes], turned[1, :rows, lanes] = split(re * cos - im * sin)
        turned[0, rows:, lanes], turned[1, rows:, lanes] = split(im * cos + re * sin)
    high, low = turned[0], turned[1]
    return dot(outer_back[0], high) + dot(outer_back[0], low) + dot(outer_back[1], high)


def multiply(a, b):
    a_re, a_im, b_re, b_im = a[:, :LANES], a[:, LANES:], b[:, :LANES], b[:, LANES:]
    return jnp.concatenate([a_re * b_re - a_im * b_im, a_re * b_im + a_im * b_re], axis=1)


def short_conv(x, taps, lane, first):
    one = pltpu.roll(x, 1, 1)
    two = pltpu.roll(x, 2, 1)
    one_up = jnp.where(first, 0.0, pltpu.roll(one, 1, 0))
    two_up = jnp.where(first, 0.0, pltpu.roll(two, 1, 0))
    one = jnp.where(lane < 1, one_up, one)
    two = jnp.where(lane < 2, two_up, two)
    return taps[0] * x + taps[1] * one + taps[2] * two


def kernel(
    peers, streams_hbm, filter_hbm, taps_hbm, skip_hbm, outer_hbm, back_hbm, inner_hbm, turn_hbm,
    out,
    taps_v, skip_v, outer, back, inner, turn,
    filter_in, pair_in, query_in, wide, gated_out, turned, filt, streams,
    load_sem, own_sem, send_sem, recv_sem,
):
    rows = 8 * peers
    channels = OWN * peers
    me = lax.axis_index("seq")
    ring_at = [lax.rem(me // 8 + d, 4) * 8 for d in range(4)]
    column_at = [lax.rem(me // 2 % 4 + d, 4) * 2 for d in range(4)]
    core_at = [lax.rem(me % 2 + d, 2) for d in range(2)]
    order = [ring_at[y] + column_at[z] + core_at[core] for y, z, core in far_first(peers)]

    barrier = pltpu.get_barrier_semaphore()
    for peer in order:
        pl.semaphore_signal(
            barrier, inc=1, device_id={"seq": peer}, device_id_type=pl.DeviceIdType.MESH
        )

    def load(i, source, target):
        copy = pltpu.make_async_copy(source, target, load_sem.at[i])
        copy.start()
        return copy

    own_loads = [load(6, streams_hbm, streams), load(7, filter_hbm, filt)]
    loads = [
        load(0, outer_hbm, outer), load(1, turn_hbm, turn), load(2, inner_hbm, inner),
        load(3, back_hbm, back), load(4, taps_hbm, taps_v), load(5, skip_hbm, skip_v),
    ]

    links = (
        (lambda p: filt.at[p // 4, :, p % 4], lambda p: filter_in.at[p]),
        (lambda p: streams.at[pl.ds(1, 2), p // 4, :, p % 4], lambda p: pair_in.at[:, p]),
        (lambda p: streams.at[0, p // 4, :, p % 4], lambda p: query_in.at[p]),
        (lambda p: gated_out.at[p], lambda p: out.at[p // 4, :, p % 4]),
    )

    def start(index, peer):
        source_of, target_of = links[index]
        pltpu.make_async_remote_copy(
            src_ref=source_of(peer),
            dst_ref=target_of(me),
            send_sem=send_sem.at[index],
            recv_sem=recv_sem.at[index],
            device_id={"seq": peer},
            device_id_type=pl.DeviceIdType.MESH,
        ).start()

    def keep(index):
        source_of, target_of = links[index]
        own = pltpu.make_async_copy(source_of(me), target_of(me), own_sem.at[index])
        own.start()
        return own

    def wait(others, sem):
        pltpu.make_async_copy(others, others, sem).wait()

    for copy in own_loads:
        copy.wait()
    owns = [keep(index) for index in range(3)]
    pl.semaphore_wait(barrier, peers - 1)
    for index in (1, 0, 2):
        for peer in order:
            start(index, peer)
    rest = pl.ds(0, peers - 1)
    for copy in loads:
        copy.wait()

    def one_channel(ref, c):
        return ref[pl.ds(c, rows, stride=OWN), :]

    lane = lax.broadcasted_iota(jnp.int32, (rows, LANES), 1)
    first = lax.broadcasted_iota(jnp.int32, (rows, LANES), 0) < 1
    channel = lax.broadcasted_iota(jnp.int32, (1, channels), 1)

    def pick(v, own):
        return jnp.sum(jnp.where(channel == own, v, 0.0), axis=1, keepdims=True)

    def shorted(ref, s):
        wide[s] = ref.reshape(OWN * rows, LANES)[...].astype(jnp.float32)
        results = []
        for c in range(OWN):
            taps = [pick(taps_v[s, i:i + 1, :], OWN * me + c) for i in range(3)]
            results.append(short_conv(one_channel(wide.at[s], c), taps, lane, first))
        return results

    owns[1].wait()
    wait(pair_in.at[:, rest], recv_sem.at[1])
    key, value = shorted(pair_in.at[0], 1), shorted(pair_in.at[1], 2)
    mixed = [k * v for k, v in zip(key, value)]
    bins = forward(jnp.concatenate(mixed, axis=1), rows, outer, inner, turn)
    owns[0].wait()
    wait(filter_in.at[rest], recv_sem.at[0])
    pairs = filter_in.reshape(OWN * rows, LANES)
    taken = jnp.concatenate([one_channel(pairs, c) for c in range(OWN)], axis=1)
    filter_bins = forward(taken, rows, outer, inner, turn)

    conv = backward(multiply(bins, filter_bins), rows, back, inner, turn, turned)

    owns[2].wait()
    wait(query_in.at[rest], recv_sem.at[2])
    query = shorted(query_in, 0)
    for c in range(OWN):
        gain = pick(skip_v[...], OWN * me + c)
        gated = query[c] * (conv[:, c * LANES:(c + 1) * LANES] + gain * mixed[c])
        wide[3, pl.ds(c, rows, stride=OWN), :] = gated
    gated_out.reshape(OWN * rows, LANES)[...] = wide[3].astype(jnp.bfloat16)
    for peer in range(2):
        pl.when(me != peer)(functools.partial(start, 3, peer))
    for peer in order:
        pl.when(peer >= 2)(functools.partial(start, 3, peer))
    own = keep(3)

    wait(filter_in.at[rest], send_sem.at[0])
    wait(pair_in.at[:, rest], send_sem.at[1])
    wait(query_in.at[rest], send_sem.at[2])
    wait(gated_out.at[rest], send_sem.at[3])
    own.wait()
    wait(gated_out.at[rest], recv_sem.at[3])


def in_pairs(x):
    lead, channels = x.shape[:-2], x.shape[-2]
    x = x.reshape(lead + (channels // 8, 8, 8, LANES))
    return jnp.swapaxes(x, -3, -2).reshape(lead + (channels // 8, 8, 4, OWN, LANES))


def out_of_pairs(x):
    groups = x.shape[0]
    x = jnp.swapaxes(x.reshape(groups, 8, 8, LANES), 1, 2)
    return x.reshape(groups * 8, 8 * LANES)


def body(streams, short_taps, long_filter, skip_gain):
    peers = lax.axis_size("seq")
    rows = 8 * peers
    outer, back, inner, turn = (jnp.asarray(t) for t in tables(rows))
    f32, bf16 = jnp.float32, jnp.bfloat16
    vmem = pltpu.VMEM
    taps = jnp.transpose(short_taps, (0, 2, 1))
    skip = skip_gain.reshape(1, -1)
    operands = (in_pairs(streams), in_pairs(long_filter), taps, skip, outer, back, inner, turn)
    anywhere = pl.BlockSpec(memory_space=pl.ANY)
    one = (peers, 8, OWN, LANES)
    result = pl.pallas_call(
        functools.partial(kernel, peers),
        out_shape=vmem((OWN * peers // 8, 8, 4, OWN, LANES), bf16),
        in_specs=[anywhere] * len(operands),
        out_specs=anywhere,
        scratch_shapes=[
            vmem(taps.shape, f32), vmem(skip.shape, f32),
            vmem(outer.shape, bf16), vmem(back.shape, bf16), vmem(inner.shape, bf16), vmem(turn.shape, f32),
            vmem(one, f32), vmem((2,) + one, bf16), vmem(one, bf16),
            vmem((4, OWN * rows, LANES), f32), vmem(one, bf16), vmem((2, 2 * rows, OWN * LANES), bf16),
            vmem(operands[1].shape, f32), vmem(operands[0].shape, bf16),
            pltpu.SemaphoreType.DMA((8,)), pltpu.SemaphoreType.DMA((4,)),
            pltpu.SemaphoreType.DMA((4,)), pltpu.SemaphoreType.DMA((4,)),
        ],
        compiler_params=pltpu.CompilerParams(
            collective_id=0, has_side_effects=True, vmem_limit_bytes=VMEM_LIMIT
        ),
    )(*(pltpu.with_memory_space_constraint(x, pltpu.HBM) for x in operands))
    return out_of_pairs(result)


def solution(mesh):
    return jax.shard_map(
        body,
        mesh=mesh,
        in_specs=(P(None, "chan", "seq"), P(None, "chan", None), P("chan", "seq"), P("chan")),
        out_specs=P("chan", "seq"),
        check_vma=False,
    )
```

time: 25.1 us -> 24.6 us (0.980)
  Pallas kernels: 24.3 us -> 23.8 us
    pallas_call x1, Pallas kernels: 24.3 us -> 23.8 us  [body(): pl.pallas_call(functools.partial(kernel, peers), out_shape=vmem((OWN * pe...]
where the time goes in v3:
time: 24.6 us; the launch traced here: 24.5 us
  Pallas kernels  23.8 us (97%)
  local copies, waits for them, and re-layouts  0.66 us (3%)
    pallas_call x1, Pallas kernels, body(): pl.pallas_call(functools.partial(kernel, peers), out_shape=vmem((OWN * pe...  23.8 us
    unnamed x1, local copies, waits for them, and re-layouts  0.66 us

profile of v3, /device:TPU:1, one launch (start us, length us, event | category | flops | bytes accessed | tf_op | source)
XLA Modules:
  0.0 24.5 jit_solution(6715958644478266413)
XLA Ops:
  0.0 23.8 %shard_map.82 = bf16[8,8,4,2,128]{4,3,2,1,0:T(2,128)(2,1)S(1)} custom-call(bf16[3,8,8,4,2,128]{5,4,3,2,1,0:T(2,128)(2,1)} %bitcast.18, f32[8,8,4,2,128]{4,3,2,1,0:T(2,128)} %bitcast.19, f32[3,3,64]{2,1,0:T(4,128)} %bitcast.20, f32[1,64]{1,0:T(1,128)} %bitcast.21, bf16[2,512,256]{2,1,0:T(8,128)(2,1)} %constant.8.clone.outer_hbm, ...), custom_call_target="tpu_custom_call" | custom-call | tf_op jit(solution)/shard_map/pallas_call | solution.py:248
  23.8 0.7 %copy.10 = bf16[64,1024]{1,0:T(8,128)(2,1)} copy(bf16[64,1024]{1,0:T(8,128)(2,1)S(1)} %bitcast.17) | data formatting | bytes 262144

commit v4 on v3

--- a/solution.py
+++ b/solution.py
@@ -35,10 +35,10 @@
     return halves(outer), halves(outer_back), np.concatenate([halves(inner), halves(inner.T)]), turn
 
 
-def far_first(peers):
+def slow_first(peers):
     steps = [(y, z, core) for y in range(max(1, peers // 8)) for z in range(min(4, peers // 2)) for core in range(2)]
-    hops = lambda step: min(step[0], 4 - step[0]) + min(step[1], 4 - step[1])
-    return sorted(steps[1:], key=hops, reverse=True)
+    toll = (0, 4.5, 6, 2)
+    return sorted(steps[2:], key=lambda step: toll[step[0]] + toll[step[1]] + 2 * (1 - step[2]), reverse=True)
 
 
 def split(x):
@@ -109,10 +109,12 @@
     rows = 8 * peers
     channels = OWN * peers
     me = lax.axis_index("seq")
-    ring_at = [lax.rem(me // 8 + d, 4) * 8 for d in range(4)]
-    column_at = [lax.rem(me // 2 % 4 + d, 4) * 2 for d in range(4)]
-    core_at = [lax.rem(me % 2 + d, 2) for d in range(2)]
-    order = [ring_at[y] + column_at[z] + core_at[core] for y, z, core in far_first(peers)]
+    y, z = me // 8, me // 2 % 4
+    to_y, to_z = (jnp.where(at >= 2, 1, 3) for at in (y, z))
+    ring_at = [lax.rem(y + to_y * d, 4) * 8 for d in range(4)]
+    column_at = [lax.rem(z + to_z * d, 4) * 2 for d in range(4)]
+    order = [ring_at[a] + column_at[b] + core for a, b, core in slow_first(peers)]
+    order.append(me + 1 - 2 * (me % 2))
 
     barrier = pltpu.get_barrier_semaphore()
     for peer in order:
@@ -126,11 +128,6 @@
         return copy
 
     own_loads = [load(6, streams_hbm, streams), load(7, filter_hbm, filt)]
-    loads = [
-        load(0, outer_hbm, outer), load(1, turn_hbm, turn), load(2, inner_hbm, inner),
-        load(3, back_hbm, back), load(4, taps_hbm, taps_v), load(5, skip_hbm, skip_v),
-    ]
-
     links = (
         (lambda p: filt.at[p // 4, :, p % 4], lambda p: filter_in.at[p]),
         (lambda p: streams.at[pl.ds(1, 2), p // 4, :, p % 4], lambda p: pair_in.at[:, p]),
@@ -165,6 +162,11 @@
     for index in (1, 0, 2):
         for peer in order:
             start(index, peer)
+    loads = [
+        load(0, outer_hbm, outer), load(1, turn_hbm, turn), load(2, inner_hbm, inner),
+        load(3, back_hbm, back), load(4, taps_hbm, taps_v), load(5, skip_hbm, skip_v),
+    ]
+
     rest = pl.ds(0, peers - 1)
     for copy in loads:
         copy.wait()
@@ -208,7 +210,7 @@
         gated = query[c] * (conv[:, c * LANES:(c + 1) * LANES] + gain * mixed[c])
         wide[3, pl.ds(c, rows, stride=OWN), :] = gated
     gated_out.reshape(OWN * rows, LANES)[...] = wide[3].astype(jnp.bfloat16)
-    for peer in range(2):
+    for peer in (1, 0):
         pl.when(me != peer)(functools.partial(start, 3, peer))
     for peer in order:
         pl.when(peer >= 2)(functools.partial(start, 3, peer))

time: 24.6 us -> 24 us (0.976)
  Pallas kernels: 23.8 us -> 23.2 us
    pallas_call x1, Pallas kernels: 23.8 us -> 23.2 us  [body(): pl.pallas_call(functools.partial(kernel, peers), out_shape=vmem((OWN * pe...]
where the time goes in v4:
time: 24 us; the launch traced here: 23.8 us
  Pallas kernels  23.2 us (97%)
  local copies, waits for them, and re-layouts  0.66 us (3%)
    pallas_call x1, Pallas kernels, body(): pl.pallas_call(functools.partial(kernel, peers), out_shape=vmem((OWN * pe...  23.2 us
    unnamed x1, local copies, waits for them, and re-layouts  0.66 us

profile of v4, /device:TPU:1, one launch (start us, length us, event | category | flops | bytes accessed | tf_op | source)
XLA Modules:
  0.0 23.8 jit_solution(9058871528882129857)
XLA Ops:
  0.0 23.2 %shard_map.82 = bf16[8,8,4,2,128]{4,3,2,1,0:T(2,128)(2,1)S(1)} custom-call(bf16[3,8,8,4,2,128]{5,4,3,2,1,0:T(2,128)(2,1)} %bitcast.18, f32[8,8,4,2,128]{4,3,2,1,0:T(2,128)} %bitcast.19, f32[3,3,64]{2,1,0:T(4,128)} %bitcast.20, f32[1,64]{1,0:T(1,128)} %bitcast.21, bf16[2,512,256]{2,1,0:T(8,128)(2,1)} %constant.8.clone.outer_hbm, ...), custom_call_target="tpu_custom_call" | custom-call | tf_op jit(solution)/shard_map/pallas_call | solution.py:250
  23.2 0.7 %copy.10 = bf16[64,1024]{1,0:T(8,128)(2,1)} copy(bf16[64,1024]{1,0:T(8,128)(2,1)S(1)} %bitcast.17) | data formatting | bytes 262144

commit v5 on v4

--- a/solution.py
+++ b/solution.py
@@ -71,7 +71,7 @@
     return right(jnp.concatenate(turned, axis=0), inner[0], inner[1])
 
 
-def backward(y, rows, outer_back, inner, turn, turned):
+def backward(y, rows, inner, turn, turned):
     part = right(y, inner[2], inner[3])
     cos, sin = turn[0], turn[1]
     for c in range(OWN):
@@ -80,8 +80,12 @@
         im = part[c * rows:(c + 1) * rows, LANES:]
         turned[0, :rows, lanes], turned[1, :rows, lanes] = split(re * cos - im * sin)
         turned[0, rows:, lanes], turned[1, rows:, lanes] = split(im * cos + re * sin)
+
+
+def last_matrix(outer_back, turned, some):
     high, low = turned[0], turned[1]
-    return dot(outer_back[0], high) + dot(outer_back[0], low) + dot(outer_back[1], high)
+    near, far = outer_back[0, :some], outer_back[1, :some]
+    return dot(near, high) + dot(near, low) + dot(far, high)
 
 
 def multiply(a, b):
@@ -141,7 +145,7 @@
             src_ref=source_of(peer),
             dst_ref=target_of(me),
             send_sem=send_sem.at[index],
-            recv_sem=recv_sem.at[index],
+            recv_sem=recv_sem.at[jnp.where(me < 2, 4, 2) if index == 2 else index],
             device_id={"seq": peer},
             device_id_type=pl.DeviceIdType.MESH,
         ).start()
@@ -151,6 +155,13 @@
         own = pltpu.make_async_copy(source_of(me), target_of(me), own_sem.at[index])
         own.start()
         return own
+
+    first_chip = me < 2
+
+    def wait_some(buffer, senders, sem):
+        mine = first_chip if senders == 2 else jnp.logical_not(first_chip)
+        for this_one, count in ((mine, senders - 1), (jnp.logical_not(mine), senders)):
+            pl.when(this_one)(functools.partial(wait, buffer.at[pl.ds(0, count)], sem))
 
     def wait(others, sem):
         pltpu.make_async_copy(others, others, sem).wait()
@@ -174,24 +185,27 @@
     def one_channel(ref, c):
         return ref[pl.ds(c, rows, stride=OWN), :]
 
-    lane = lax.broadcasted_iota(jnp.int32, (rows, LANES), 1)
-    first = lax.broadcasted_iota(jnp.int32, (rows, LANES), 0) < 1
     channel = lax.broadcasted_iota(jnp.int32, (1, channels), 1)
 
     def pick(v, own):
         return jnp.sum(jnp.where(channel == own, v, 0.0), axis=1, keepdims=True)
 
-    def shorted(ref, s):
-        wide[s] = ref.reshape(OWN * rows, LANES)[...].astype(jnp.float32)
-        results = []
-        for c in range(OWN):
-            taps = [pick(taps_v[s, i:i + 1, :], OWN * me + c) for i in range(3)]
-            results.append(short_conv(one_channel(wide.at[s], c), taps, lane, first))
-        return results
+    taps = [
+        [[pick(taps_v[s, i:i + 1, :], OWN * me + c) for i in range(3)] for c in range(OWN)] for s in range(3)
+    ]
+    gains = [pick(skip_v[...], OWN * me + c) for c in range(OWN)]
+
+    def shorted(ref, s, some):
+        lane = lax.broadcasted_iota(jnp.int32, (some, LANES), 1)
+        first = lax.broadcasted_iota(jnp.int32, (some, LANES), 0) < 1
+        wide[s, :OWN * some] = ref.reshape(OWN * rows, LANES)[:OWN * some].astype(jnp.float32)
+        return [
+            short_conv(wide[s, pl.ds(c, some, stride=OWN), :], taps[s][c], lane, first) for c in range(OWN)
+        ]
 
     owns[1].wait()
     wait(pair_in.at[:, rest], recv_sem.at[1])
-    key, value = shorted(pair_in.at[0], 1), shorted(pair_in.at[1], 2)
+    key, value = shorted(pair_in.at[0], 1, rows), shorted(pair_in.at[1], 2, rows)
     mixed = [k * v for k, v in zip(key, value)]
     bins = forward(jnp.concatenate(mixed, axis=1), rows, outer, inner, turn)
     owns[0].wait()
@@ -200,18 +214,29 @@
     taken = jnp.concatenate([one_channel(pairs, c) for c in range(OWN)], axis=1)
     filter_bins = forward(taken, rows, outer, inner, turn)
 
-    conv = backward(multiply(bins, filter_bins), rows, back, inner, turn, turned)
-
+    backward(multiply(bins, filter_bins), rows, inner, turn, turned)
+
+    def ungated(some):
+        conv = last_matrix(back, turned, some)
+        return [conv[:, c * LANES:(c + 1) * LANES] + gains[c] * mixed[c][:some] for c in range(OWN)]
+
+    def gate(values, begin, end):
+        query = shorted(query_in, 0, end)
+        for c in range(OWN):
+            wide[3, pl.ds(c, end, stride=OWN), :] = query[c] * values[c]
+        cut = pl.ds(OWN * begin, OWN * (end - begin))
+        gated_out.reshape(OWN * rows, LANES)[cut] = wide[3, cut].astype(jnp.bfloat16)
+
+    ahead = 16
+    values = ungated(ahead)
     owns[2].wait()
-    wait(query_in.at[rest], recv_sem.at[2])
-    query = shorted(query_in, 0)
-    for c in range(OWN):
-        gain = pick(skip_v[...], OWN * me + c)
-        gated = query[c] * (conv[:, c * LANES:(c + 1) * LANES] + gain * mixed[c])
-        wide[3, pl.ds(c, rows, stride=OWN), :] = gated
-    gated_out.reshape(OWN * rows, LANES)[...] = wide[3].astype(jnp.bfloat16)
+    wait_some(query_in, 2, recv_sem.at[4])
+    gate(values, 0, ahead)
     for peer in (1, 0):
         pl.when(me != peer)(functools.partial(start, 3, peer))
+    wait_some(query_in, peers - 2, recv_sem.at[2])
+    all_values = ungated(rows)
+    gate(all_values, ahead, rows)
     for peer in order:
         pl.when(peer >= 2)(functools.partial(start, 3, peer))
     own = keep(3)
@@ -259,7 +284,7 @@
             vmem((4, OWN * rows, LANES), f32), vmem(one, bf16), vmem((2, 2 * rows, OWN * LANES), bf16),
             vmem(operands[1].shape, f32), vmem(operands[0].shape, bf16),
             pltpu.SemaphoreType.DMA((8,)), pltpu.SemaphoreType.DMA((4,)),
-            pltpu.SemaphoreType.DMA((4,)), pltpu.SemaphoreType.DMA((4,)),
+            pltpu.SemaphoreType.DMA((4,)), pltpu.SemaphoreType.DMA((5,)),
         ],
         compiler_params=pltpu.CompilerParams(
             collective_id=0, has_side_effects=True, vmem_limit_bytes=VMEM_LIMIT

time: 24 us -> 23.5 us (0.979)
  Pallas kernels: 23.2 us -> 22.7 us
    pallas_call x1, Pallas kernels: 23.2 us -> 22.7 us  [body(): pl.pallas_call(functools.partial(kernel, peers), out_shape=vmem((OWN * pe...]
where the time goes in v5:
time: 23.5 us; the launch traced here: 23.3 us
  Pallas kernels  22.7 us (97%)
  local copies, waits for them, and re-layouts  0.66 us (3%)
    pallas_call x1, Pallas kernels, body(): pl.pallas_call(functools.partial(kernel, peers), out_shape=vmem((OWN * pe...  22.7 us
    unnamed x1, local copies, waits for them, and re-layouts  0.66 us

profile of v5, /device:TPU:1, one launch (start us, length us, event | category | flops | bytes accessed | tf_op | source)
XLA Modules:
  0.0 23.3 jit_solution(18162821172950071969)
XLA Ops:
  0.0 22.7 %shard_map.82 = bf16[8,8,4,2,128]{4,3,2,1,0:T(2,128)(2,1)S(1)} custom-call(bf16[3,8,8,4,2,128]{5,4,3,2,1,0:T(2,128)(2,1)} %bitcast.18, f32[8,8,4,2,128]{4,3,2,1,0:T(2,128)} %bitcast.19, f32[3,3,64]{2,1,0:T(4,128)} %bitcast.20, f32[1,64]{1,0:T(1,128)} %bitcast.21, bf16[2,512,256]{2,1,0:T(8,128)(2,1)} %constant.8.clone.outer_hbm, ...), custom_call_target="tpu_custom_call" | custom-call | tf_op jit(solution)/shard_map/pallas_call | solution.py:275
  22.7 0.7 %copy.10 = bf16[64,1024]{1,0:T(8,128)(2,1)} copy(bf16[64,1024]{1,0:T(8,128)(2,1)S(1)} %bitcast.17) | data formatting | bytes 262144

commit v6 on v5

--- a/solution.py
+++ b/solution.py
@@ -37,8 +37,8 @@
 
 def slow_first(peers):
     steps = [(y, z, core) for y in range(max(1, peers // 8)) for z in range(min(4, peers // 2)) for core in range(2)]
-    toll = (0, 4.5, 6, 2)
-    return sorted(steps[2:], key=lambda step: toll[step[0]] + toll[step[1]] + 2 * (1 - step[2]), reverse=True)
+    toll = (0, 3.5, 6, 2.5)
+    return sorted(steps[2:], key=lambda step: toll[step[0]] + toll[step[1]] + 3 * (1 - step[2]), reverse=True)
 
 
 def split(x):
@@ -131,7 +131,11 @@
         copy.start()
         return copy
 
-    own_loads = [load(6, streams_hbm, streams), load(7, filter_hbm, filt)]
+    own_loads = [
+        load(6, streams_hbm.at[pl.ds(1, 2)], streams.at[pl.ds(1, 2)]),
+        load(7, filter_hbm, filt),
+        load(8, streams_hbm.at[0], streams.at[0]),
+    ]
     links = (
         (lambda p: filt.at[p // 4, :, p % 4], lambda p: filter_in.at[p]),
         (lambda p: streams.at[pl.ds(1, 2), p // 4, :, p % 4], lambda p: pair_in.at[:, p]),
@@ -166,13 +170,12 @@
     def wait(others, sem):
         pltpu.make_async_copy(others, others, sem).wait()
 
-    for copy in own_loads:
-        copy.wait()
-    owns = [keep(index) for index in range(3)]
     pl.semaphore_wait(barrier, peers - 1)
-    for index in (1, 0, 2):
+    for index, own_load in zip((1, 0, 2), own_loads):
+        own_load.wait()
         for peer in order:
             start(index, peer)
+    owns = [keep(index) for index in range(3)]
     loads = [
         load(0, outer_hbm, outer), load(1, turn_hbm, turn), load(2, inner_hbm, inner),
         load(3, back_hbm, back), load(4, taps_hbm, taps_v), load(5, skip_hbm, skip_v),
@@ -283,7 +286,7 @@
             vmem(one, f32), vmem((2,) + one, bf16), vmem(one, bf16),
             vmem((4, OWN * rows, LANES), f32), vmem(one, bf16), vmem((2, 2 * rows, OWN * LANES), bf16),
             vmem(operands[1].shape, f32), vmem(operands[0].shape, bf16),
-            pltpu.SemaphoreType.DMA((8,)), pltpu.SemaphoreType.DMA((4,)),
+            pltpu.SemaphoreType.DMA((9,)), pltpu.SemaphoreType.DMA((4,)),
             pltpu.SemaphoreType.DMA((4,)), pltpu.SemaphoreType.DMA((5,)),
         ],
         compiler_params=pltpu.CompilerParams(

time: 23.5 us -> 23.4 us (level)
  no operation moved by 1% of the time
where the time goes in v6:
time: 23.4 us; the launch traced here: 23.3 us
  Pallas kernels  22.6 us (97%)
  local copies, waits for them, and re-layouts  0.66 us (3%)
    pallas_call x1, Pallas kernels, body(): pl.pallas_call(functools.partial(kernel, peers), out_shape=vmem((OWN * pe...  22.6 us
    unnamed x1, local copies, waits for them, and re-layouts  0.66 us

profile of v6, /device:TPU:1, one launch (start us, length us, event | category | flops | bytes accessed | tf_op | source)
XLA Modules:
  0.0 23.3 jit_solution(828375690053527727)
XLA Ops:
  0.0 22.6 %shard_map.82 = bf16[8,8,4,2,128]{4,3,2,1,0:T(2,128)(2,1)S(1)} custom-call(bf16[3,8,8,4,2,128]{5,4,3,2,1,0:T(2,128)(2,1)} %bitcast.18, f32[8,8,4,2,128]{4,3,2,1,0:T(2,128)} %bitcast.19, f32[3,3,64]{2,1,0:T(4,128)} %bitcast.20, f32[1,64]{1,0:T(1,128)} %bitcast.21, bf16[2,512,256]{2,1,0:T(8,128)(2,1)} %constant.8.clone.outer_hbm, ...), custom_call_target="tpu_custom_call" | custom-call | tf_op jit(solution)/shard_map/pallas_call | solution.py:278
  22.6 0.7 %copy.10 = bf16[64,1024]{1,0:T(8,128)(2,1)} copy(bf16[64,1024]{1,0:T(8,128)(2,1)S(1)} %bitcast.17) | data formatting | bytes 262144

commit v7 on v6

--- a/solution.py
+++ b/solution.py
@@ -85,7 +85,8 @@
 def last_matrix(outer_back, turned, some):
     high, low = turned[0], turned[1]
     near, far = outer_back[0, :some], outer_back[1, :some]
-    return dot(near, high) + dot(near, low) + dot(far, high)
+    both = dot(jnp.concatenate([near, far], axis=0), high)
+    return both[:some] + dot(near, low) + both[some:]
 
 
 def multiply(a, b):
@@ -171,10 +172,22 @@
         pltpu.make_async_copy(others, others, sem).wait()
 
     pl.semaphore_wait(barrier, peers - 1)
-    for index, own_load in zip((1, 0, 2), own_loads):
-        own_load.wait()
-        for peer in order:
-            start(index, peer)
+    own_loads[0].wait()
+    for peer in order:
+        start(1, peer)
+    own_loads[1].wait()
+    own_loads[2].wait()
+    slow, quick = order[:22], order[22:]
+    for peer in slow:
+        start(0, peer)
+    for peer in slow:
+        pl.when(first_chip)(functools.partial(start, 2, peer))
+    for peer in quick:
+        start(0, peer)
+    for peer in slow:
+        pl.when(jnp.logical_not(first_chip))(functools.partial(start, 2, peer))
+    for peer in quick:
+        start(2, peer)
     owns = [keep(index) for index in range(3)]
     loads = [
         load(0, outer_hbm, outer), load(1, turn_hbm, turn), load(2, inner_hbm, inner),

time: 23.4 us -> 23.3 us (level)
  no operation moved by 1% of the time
where the time goes in v7:
time: 23.3 us; the launch traced here: 23.2 us
  Pallas kernels  22.5 us (97%)
  local copies, waits for them, and re-layouts  0.66 us (3%)
    pallas_call x1, Pallas kernels, body(): pl.pallas_call(functools.partial(kernel, peers), out_shape=vmem((OWN * pe...  22.5 us
    unnamed x1, local copies, waits for them, and re-layouts  0.66 us

profile of v7, /device:TPU:1, one launch (start us, length us, event | category | flops | bytes accessed | tf_op | source)
XLA Modules:
  0.0 23.2 jit_solution(13622625338982352167)
XLA Ops:
  0.0 22.5 %shard_map.82 = bf16[8,8,4,2,128]{4,3,2,1,0:T(2,128)(2,1)S(1)} custom-call(bf16[3,8,8,4,2,128]{5,4,3,2,1,0:T(2,128)(2,1)} %bitcast.18, f32[8,8,4,2,128]{4,3,2,1,0:T(2,128)} %bitcast.19, f32[3,3,64]{2,1,0:T(4,128)} %bitcast.20, f32[1,64]{1,0:T(1,128)} %bitcast.21, bf16[2,512,256]{2,1,0:T(8,128)(2,1)} %constant.8.clone.outer_hbm, ...), custom_call_target="tpu_custom_call" | custom-call | tf_op jit(solution)/shard_map/pallas_call | solution.py:291
  22.5 0.7 %copy.10 = bf16[64,1024]{1,0:T(8,128)(2,1)} copy(bf16[64,1024]{1,0:T(8,128)(2,1)S(1)} %bitcast.17) | data formatting | bytes 262144

commit v8 on v7

--- a/solution.py
+++ b/solution.py
@@ -122,11 +122,6 @@
     order.append(me + 1 - 2 * (me % 2))
 
     barrier = pltpu.get_barrier_semaphore()
-    for peer in order:
-        pl.semaphore_signal(
-            barrier, inc=1, device_id={"seq": peer}, device_id_type=pl.DeviceIdType.MESH
-        )
-
     def load(i, source, target):
         copy = pltpu.make_async_copy(source, target, load_sem.at[i])
         copy.start()
@@ -137,6 +132,12 @@
         load(7, filter_hbm, filt),
         load(8, streams_hbm.at[0], streams.at[0]),
     ]
+
+    for peer in order:
+        pl.semaphore_signal(
+            barrier, inc=1, device_id={"seq": peer}, device_id_type=pl.DeviceIdType.MESH
+        )
+
     links = (
         (lambda p: filt.at[p // 4, :, p % 4], lambda p: filter_in.at[p]),
         (lambda p: streams.at[pl.ds(1, 2), p // 4, :, p % 4], lambda p: pair_in.at[:, p]),

time: 23.3 us -> 23.3 us (level)
  no operation moved by 1% of the time
where the time goes in v8:
time: 23.3 us; the launch traced here: 23.2 us
  Pallas kernels  22.5 us (97%)
  local copies, waits for them, and re-layouts  0.66 us (3%)
    pallas_call x1, Pallas kernels, body(): pl.pallas_call(functools.partial(kernel, peers), out_shape=vmem((OWN * pe...  22.5 us
    unnamed x1, local copies, waits for them, and re-layouts  0.66 us

profile of v8, /device:TPU:1, one launch (start us, length us, event | category | flops | bytes accessed | tf_op | source)
XLA Modules:
  0.0 23.2 jit_solution(5070353258480633020)
XLA Ops:
  0.0 22.5 %shard_map.82 = bf16[8,8,4,2,128]{4,3,2,1,0:T(2,128)(2,1)S(1)} custom-call(bf16[3,8,8,4,2,128]{5,4,3,2,1,0:T(2,128)(2,1)} %bitcast.18, f32[8,8,4,2,128]{4,3,2,1,0:T(2,128)} %bitcast.19, f32[3,3,64]{2,1,0:T(4,128)} %bitcast.20, f32[1,64]{1,0:T(1,128)} %bitcast.21, bf16[2,512,256]{2,1,0:T(8,128)(2,1)} %constant.8.clone.outer_hbm, ...), custom_call_target="tpu_custom_call" | custom-call | tf_op jit(solution)/shard_map/pallas_call | solution.py:292
  22.5 0.7 %copy.10 = bf16[64,1024]{1,0:T(8,128)(2,1)} copy(bf16[64,1024]{1,0:T(8,128)(2,1)S(1)} %bitcast.17) | data formatting | bytes 262144

commit v9 on v8

--- a/solution.py
+++ b/solution.py
@@ -178,7 +178,7 @@
         start(1, peer)
     own_loads[1].wait()
     own_loads[2].wait()
-    slow, quick = order[:22], order[22:]
+    slow, quick = order[:26], order[26:]
     for peer in slow:
         start(0, peer)
     for peer in slow:

time: 23.3 us -> 23.3 us (level)
  no operation moved by 1% of the time
where the time goes in v9:
time: 23.3 us; the launch traced here: 23.2 us
  Pallas kernels  22.5 us (97%)
  local copies, waits for them, and re-layouts  0.66 us (3%)
    pallas_call x1, Pallas kernels, body(): pl.pallas_call(functools.partial(kernel, peers), out_shape=vmem((OWN * pe...  22.5 us
    unnamed x1, local copies, waits for them, and re-layouts  0.66 us

profile of v9, /device:TPU:1, one launch (start us, length us, event | category | flops | bytes accessed | tf_op | source)
XLA Modules:
  0.0 23.2 jit_solution(18027488680450666909)
XLA Ops:
  0.0 22.5 %shard_map.82 = bf16[8,8,4,2,128]{4,3,2,1,0:T(2,128)(2,1)S(1)} custom-call(bf16[3,8,8,4,2,128]{5,4,3,2,1,0:T(2,128)(2,1)} %bitcast.18, f32[8,8,4,2,128]{4,3,2,1,0:T(2,128)} %bitcast.19, f32[3,3,64]{2,1,0:T(4,128)} %bitcast.20, f32[1,64]{1,0:T(1,128)} %bitcast.21, bf16[2,512,256]{2,1,0:T(8,128)(2,1)} %constant.8.clone.outer_hbm, ...), custom_call_target="tpu_custom_call" | custom-call | tf_op jit(solution)/shard_map/pallas_call | solution.py:292
  22.5 0.7 %copy.10 = bf16[64,1024]{1,0:T(8,128)(2,1)} copy(bf16[64,1024]{1,0:T(8,128)(2,1)S(1)} %bitcast.17) | data formatting | bytes 262144
